TPU v7x, 512 devices: a whole 4x4x16 slice. The times are simulated.
512 devices in a mesh: row: 16 (over z), col: 32 (over x, y, core).
Axes of the slice: x: 4, y: 4, z: 16, core: 2. Of those that a mesh axis runs over, the one named last changes fastest.
Arguments:
- inverse_top: bfloat16 [4096, 4096], P('col', 'row'), may hold values from -0.09375 to 0.09375
- inverse_one: bfloat16 [6144, 3072], P('col', 'row'), may hold values from -0.109375 to 0.109375
- inverse_two: bfloat16 [8192, 2048], P('col', 'row'), may hold values from -0.125 to 0.125
- inverse_leaf: bfloat16 [8192, 1024], P('col', 'row'), may hold values from -0.1875 to 0.1875
- coupling_one: bfloat16 [3072, 6144], P('row', 'col'), may hold values from -0.109375 to 0.109375
- coupling_two: bfloat16 [2048, 8192], P('row', 'col'), may hold values from -0.125 to 0.125
- coupling_leaf: bfloat16 [1024, 8192], P('row', 'col'), may hold values from -0.1875 to 0.1875
- rhs_top: bfloat16 [4096, 256], P('row', 'col'), may hold values from -6 to 6
- rhs_one: bfloat16 [3072, 512], P('row', 'col'), may hold values from -6 to 6
- rhs_two: bfloat16 [2048, 1024], P('row', 'col'), may hold values from -6 to 6
- rhs_leaf: bfloat16 [1024, 2048], P('row', 'col'), may hold values from -6 to 6
- parent_map_one: int32 [2, 3072], replicated, may hold values from 0 to 4095, as said below
- parent_map_two: int32 [4, 2048], replicated, may hold values from 0 to 6143, as said below
- parent_map_leaf: int32 [8, 1024], replicated, may hold values from 0 to 4095, as said below
Outputs:
- solution_top: bfloat16 [4096, 256], P('row', 'col')
- solution_one: bfloat16 [3072, 512], P('row', 'col')
- solution_two: bfloat16 [2048, 1024], P('row', 'col')
- solution_leaf: bfloat16 [1024, 2048], P('row', 'col')
Inputs may be any that keep to these rules, and one draw needn't show every extreme that they name: `parent_map_one`: row k lists distinct rows of the top front, one for each of the 3072 update rows of front k. Cut the update rows and the top separator each into 16 equal blocks: at most 24 rows of one block land in one block of the top front, a number that is reached in every row, and every block of the top front receives exactly 192 rows from each child. `parent_map_two`: row k lists distinct rows of the front k // 2 of the second level (its 3072 separator rows first, then its 3072 update rows), one for each of the 2048 update rows of front k. Cut the update rows into 16 equal blocks, and the parent's separator rows and its update rows each into 16 equal blocks, block j of the parent being the j-th separator block with the j-th update block: at most 16 rows of one block land in one parent block, reached in every row, and every parent block receives exactly 128 rows from each child. `parent_map_leaf`: as for parent_map_two, one level lower: 1024 update rows of front k into front k // 2 of the third level, at most 8 rows of one block into one parent block, reached in every row, and exactly 64 rows from each child into every parent block.
All inputs are finite; a program needn't handle non-finite values.
Results may differ from a plain program's by a relative error of at most 0.03.
Values may be sent and summed in bfloat16 or wider, within the bound.
No kernel may reach another device: no remote copies, remote signals or barrier semaphores. Data moves between devices by JAX's collectives and lax.ppermute only.
A program may use at most 64 MiB of HBM per device.

v0:
```python
import jax
import jax.numpy as jnp
from jax import lax
from jax.sharding import PartitionSpec as P


def swapped(value, axis, stride):
    mask = 2**stride
    pairs = [(source, source ^ mask) for source in range(lax.axis_size(axis))]
    return lax.ppermute(value, axis, pairs)


def route_tables(mapping, child_index, parent_sep, parent_upd, strips, row_index):
    positions = lax.dynamic_index_in_dim(mapping, child_index, 0, keepdims=False)
    sep_rows = parent_sep // strips
    in_separator = positions < parent_sep
    if parent_upd > 0:
        upd_rows = parent_upd // strips
        target = jnp.where(
            in_separator, positions // sep_rows, (positions - parent_sep) // upd_rows
        )
        offset = jnp.where(
            in_separator, positions % sep_rows, sep_rows + (positions - parent_sep) % upd_rows
        )
    else:
        target = positions // sep_rows
        offset = positions % sep_rows
    block_rows = positions.shape[0] // strips
    blocks = target.reshape(strips, block_rows)
    matches = (blocks[:, :, None] == jnp.arange(strips, dtype=jnp.int32)[None, None, :]).astype(
        jnp.int32
    )
    slot_of = jnp.sum((jnp.cumsum(matches, axis=1) - 1) * matches, axis=2).reshape(-1)
    block_len = sep_rows + parent_upd // strips
    capacity = 2 * positions.shape[0] // (strips * strips)
    source = jnp.arange(positions.shape[0], dtype=jnp.int32) // block_rows
    mine_here = target == row_index
    column_at = jnp.where(mine_here, slot_of, capacity)
    lookup = jnp.full((strips, capacity + 1), block_len, jnp.int32)
    lookup = lookup.at[source, column_at].set(jnp.where(mine_here, offset, block_len))[:, :capacity]
    local_target = lax.dynamic_slice_in_dim(target, row_index * block_rows, block_rows)
    local_slots = lax.dynamic_slice_in_dim(slot_of, row_index * block_rows, block_rows)
    return (local_target, local_slots, lookup, capacity, block_len)


def pack_rows(values, local_target, local_slots, strips, capacity):
    buffer = jnp.zeros((strips, capacity, values.shape[1]), values.dtype)
    return buffer.at[local_target, local_slots].set(values)


def unpack_rows(received, lookup, block_len):
    summed = jnp.zeros((block_len + 1, received.shape[2]), jnp.float32)
    return summed.at[lookup].add(received.astype(jnp.float32))[:block_len]


def spread(portion, depth_bits, pass_on, column):
    for bit_index in range(depth_bits):
        partner = pass_on(portion, bit_index)
        is_upper = column >> bit_index & 1 == 1
        portion = jnp.where(
            is_upper,
            jnp.concatenate([partner, portion], axis=-1),
            jnp.concatenate([portion, partner], axis=-1),
        )
    return portion


def shrink(entire, depth_bits, pass_on, column):
    for bit_index in reversed(range(depth_bits)):
        half_width = entire.shape[-1] // 2
        low_part = entire[..., :half_width]
        high_part = entire[..., half_width:]
        is_upper = column >> bit_index & 1 == 1
        kept_part = jnp.where(is_upper, high_part, low_part)
        sent_part = jnp.where(is_upper, low_part, high_part)
        entire = kept_part + pass_on(sent_part, bit_index)
    return entire


def per_device(
    inverse_top,
    inverse_one,
    inverse_two,
    inverse_leaf,
    coupling_one,
    coupling_two,
    coupling_leaf,
    rhs_top,
    rhs_one,
    rhs_two,
    rhs_leaf,
    parent_map_one,
    parent_map_two,
    parent_map_leaf,
):
    strips = lax.axis_size("row")
    col_count = lax.axis_size("col")
    row_here = lax.axis_index("row")
    column = lax.axis_index("col")
    inverses = [inverse_top, inverse_one, inverse_two, inverse_leaf]
    couplings = [None, coupling_one, coupling_two, coupling_leaf]
    right_sides = [rhs_top, rhs_one, rhs_two, rhs_leaf]
    parent_maps = [None, parent_map_one, parent_map_two, parent_map_leaf]
    orders = [inverse.shape[1] * strips for inverse in inverses]
    groups = [col_count >> tree_level for tree_level in range(4)]
    group_bits = [group_size.bit_length() - 1 for group_size in groups]
    pass_rhs = lambda values, bit_index: swapped(values, "col", bit_index)
    pass_update_sum = lambda values, bit_index: swapped(
        values.astype(jnp.bfloat16), "col", bit_index
    ).astype(values.dtype)
    pass_update_spread = lambda values, bit_index: swapped(values, "col", bit_index)
    pass_solution_sum = lambda values, bit_index: swapped(
        values.astype(jnp.bfloat16), "col", bit_index
    ).astype(values.dtype)
    pass_solution_spread = lambda values, bit_index: swapped(values, "col", bit_index)
    full_rhs = [
        spread(right_sides[tree_level], group_bits[tree_level], pass_rhs, column)
        for tree_level in range(4)
    ]
    own_routes = [None]
    sibling_routes = [None]
    for tree_level in range(1, 4):
        parent_order = orders[tree_level - 1]
        parent_update = parent_order if tree_level > 1 else 0
        front_here = column // groups[tree_level]
        own_routes.append(
            route_tables(
                parent_maps[tree_level], front_here, parent_order, parent_update, strips, row_here
            )
        )
        sibling_routes.append(
            route_tables(
                parent_maps[tree_level],
                front_here ^ 1,
                parent_order,
                parent_update,
                strips,
                row_here,
            )
        )
    pivots = [None] * 4
    incoming = None
    for tree_level in (3, 2, 1, 0):
        sep_rows = inverses[tree_level].shape[1]
        if incoming is None:
            separator = full_rhs[tree_level]
            own_update = None
        else:
            separator = (full_rhs[tree_level].astype(jnp.float32) + incoming[:sep_rows]).astype(
                jnp.bfloat16
            )
            own_update = lax.optimization_barrier(incoming[sep_rows:].astype(jnp.bfloat16))
        partial_value = jnp.dot(inverses[tree_level], separator, preferred_element_type=jnp.float32)
        solved = lax.psum(partial_value.astype(jnp.bfloat16), "row")
        pivots[tree_level] = solved
        if tree_level > 0:
            coupled = jnp.dot(couplings[tree_level], solved, preferred_element_type=jnp.float32)
            reduced = shrink(coupled, group_bits[tree_level], pass_update_sum, column)
            if own_update is None:
                portion = (-reduced).astype(jnp.bfloat16)
            else:
                start_at = column % groups[tree_level] * reduced.shape[1]
                kept_rows = lax.dynamic_slice_in_dim(own_update, start_at, reduced.shape[1], 1)
                portion = (kept_rows.astype(jnp.float32) - reduced).astype(jnp.bfloat16)
            updated = spread(portion, group_bits[tree_level], pass_update_spread, column)
            own_target, own_slots, own_lookup, capacity, block_len = own_routes[tree_level]
            partner = swapped(updated, "col", group_bits[tree_level])
            sib_target, sib_slots, sib_lookup = sibling_routes[tree_level][:3]
            got_own, got_sibling = (
                lax.all_to_all(
                    pack_rows(updated, own_target, own_slots, strips, capacity),
                    "row",
                    split_axis=0,
                    concat_axis=0,
                    tiled=True,
                ),
                lax.all_to_all(
                    pack_rows(partner, sib_target, sib_slots, strips, capacity),
                    "row",
                    split_axis=0,
                    concat_axis=0,
                    tiled=True,
                ),
            )
            incoming = unpack_rows(got_own, own_lookup, block_len) + unpack_rows(
                got_sibling, sib_lookup, block_len
            )
    solutions = [None] * 4
    parent_solution = None
    parent_gathered = None
    for tree_level in range(4):
        solved = pivots[tree_level]
        gathered = None
        if tree_level == 0:
            residual = solved
        else:
            own_target, own_slots, own_lookup, capacity, block_len = own_routes[tree_level]
            pieces = [parent_solution]
            if parent_gathered is not None:
                pieces.append(parent_gathered)
            pieces.append(jnp.zeros((1, parent_solution.shape[1]), jnp.bfloat16))
            parent_rows = jnp.concatenate(pieces, axis=0)
            returned = lax.all_to_all(
                parent_rows[own_lookup], "row", split_axis=0, concat_axis=0, tiled=True
            )
            gathered = returned[own_target, own_slots]
            coupling_term = jnp.dot(
                couplings[tree_level].T, gathered, preferred_element_type=jnp.float32
            )
            residual = (
                solved.astype(jnp.float32)
                - lax.psum(coupling_term.astype(jnp.bfloat16), "row").astype(jnp.float32)
            ).astype(jnp.bfloat16)
        contribution = jnp.dot(inverses[tree_level].T, residual, preferred_element_type=jnp.float32)
        if tree_level == 0:
            summed = lax.psum(contribution.astype(jnp.bfloat16), "col")
            solution = summed
            rhs_width = solution.shape[1] // groups[0]
            solutions[0] = lax.dynamic_slice_in_dim(
                solution, column % groups[0] * rhs_width, rhs_width, 1
            )
        else:
            portion = shrink(
                contribution, group_bits[tree_level], pass_solution_sum, column
            ).astype(jnp.bfloat16)
            solutions[tree_level] = portion
            if tree_level < 3:
                solution = spread(portion, group_bits[tree_level], pass_solution_spread, column)
        parent_solution = solution
        parent_gathered = gathered
    return (solutions[0], solutions[1], solutions[2], solutions[3])


def solution(mesh):
    in_specs = (
        P("col", "row"),
        P("col", "row"),
        P("col", "row"),
        P("col", "row"),
        P("row", "col"),
        P("row", "col"),
        P("row", "col"),
        P("row", "col"),
        P("row", "col"),
        P("row", "col"),
        P("row", "col"),
        P(),
        P(),
        P(),
    )
    out_specs = (P("row", "col"), P("row", "col"), P("row", "col"), P("row", "col"))
    return jax.shard_map(
        per_device, mesh=mesh, in_specs=in_specs, out_specs=out_specs, check_vma=False
    )
```

profile of v0, /device:TPU:1, one launch (start us, length us, event | category | flops | bytes accessed | tf_op | source)
XLA Modules:
  0.0 1660.7 jit_solution(15482872862704650823)
XLA Ops:
  7.2 8.8 collective-permute-start.5
  37.4 9.1 reduce-window.14
  54.5 124.7 %all-reduce.12.cloned.1.call-done = bf16[256,256]{0,1:T(8,128)(2,1)} async-done(((bf16[256,256]{0,1:T(8,128)(2,1)}), bf16[256,256]{0,1:T(8,128)(2,1)}) %all-reduce.12.cloned.1.call-update) | async-done | bytes 131088 | tf_op jit(solution)/shard_map/psum | solution.py:154
  185.4 12.4 collective-permute-start.8
  238.0 7.7 scatter_fusion.1
  245.7 11.4 all-to-all-start.1
  261.3 9.1 reduce-window.16
  275.6 127.5 %all-reduce.14.cloned.1.call-done = bf16[256,256]{0,1:T(8,128)(2,1)} async-done(((bf16[256,256]{0,1:T(8,128)(2,1)}), bf16[256,256]{0,1:T(8,128)(2,1)}) %all-reduce.14.cloned.1.call-update) | async-done | bytes 131088 | tf_op jit(solution)/shard_map/psum | solution.py:154
  415.0 13.9 collective-permute-start.17
  432.0 8.0 scatter_custom_fusion.13
  449.4 8.0 scatter_custom_fusion.16
  458.3 14.9 scatter_fusion.2
  486.9 14.8 scatter_fusion.3
  501.7 11.7 all-to-all-start.3
  534.6 128.2 %all-reduce.16.cloned.1.call-done = bf16[192,256]{1,0:T(8,128)(2,1)} async-done(((bf16[192,256]{1,0:T(8,128)(2,1)}), bf16[192,256]{1,0:T(8,128)(2,1)}) %all-reduce.16.cloned.1.call-update) | async-done | bytes 98320 | tf_op jit(solution)/shard_map/psum | solution.py:154
  680.8 15.2 collective-permute-start.29
  717.2 22.2 %scatter_fusion.4 = bf16[16,24,256]{2,1,0:T(8,128)(2,1)} fusion(bf16[16,24,256]{2,1,0:T(8,128)(2,1)} %broadcast.1392.clone.1, s32[192]{0:T(256)S(1)} %bitcast.300, bf16[192,256]{1,0:T(8,128)(2,1)S(1)} %maximum_select_fusion.4), kind=kCustom, calls=%fused_computation.14 | custom fusion | bytes 296448 | tf_op jit(solution)/shard_map/scatter | solution.py:48
  761.2 22.3 %scatter_fusion.5 = bf16[16,24,256]{2,1,0:T(8,128)(2,1)} fusion(bf16[16,24,256]{2,1,0:T(8,128)(2,1)} %broadcast.1392.clone, s32[192]{0:T(256)S(1)} %bitcast.299, bf16[192,256]{1,0:T(8,128)(2,1)S(1)} %collective-permute-done.34), kind=kCustom, calls=%fused_computation.16 | custom fusion | bytes 296448 | tf_op jit(solution)/shard_map/scatter | solution.py:48
  783.5 11.7 all-to-all-start.5
  795.2 11.8 scatter_custom_fusion.12
  809.4 11.8 scatter_custom_fusion.17
  832.2 126.9 %all-reduce.18.cloned.1.call-done = bf16[128,256]{0,1:T(8,128)(2,1)} async-done(((bf16[128,256]{0,1:T(8,128)(2,1)}), bf16[128,256]{0,1:T(8,128)(2,1)}) %all-reduce.18.cloned.1.call-update) | async-done | bytes 65552 | tf_op jit(solution)/shard_map/psum | solution.py:154
  960.8 138.6 %all-reduce.20.cloned.1.call-done = bf16[256,256]{0,1:T(8,128)(2,1)} async-done(((bf16[256,256]{0,1:T(8,128)(2,1)}), bf16[256,256]{0,1:T(8,128)(2,1)}) %all-reduce.20.cloned.1.call-update) | async-done | bytes 131088 | tf_op jit(solution)/shard_map/psum | solution.py:216
  1102.5 24.2 %all_to_all.45 = bf16[16,24,256]{2,1,0:T(8,128)(2,1)S(1)} all-to-all(bf16[16,24,256]{2,1,0:T(8,128)(2,1)S(1)} %bitcast.302), channel_id=1, replica_groups=mesh['row'=16,'col'=32] {'row'}, dimensions={0} | all-to-all | bytes 393216 | tf_op jit(solution)/shard_map/all_to_all | solution.py:203
  1130.0 121.3 %all-reduce.22.cloned.1.call-done = bf16[192,256]{1,0:T(8,128)(2,1)} async-done(((bf16[192,256]{1,0:T(8,128)(2,1)}), bf16[192,256]{1,0:T(8,128)(2,1)}) %all-reduce.22.cloned.1.call-update) | async-done | bytes 98320 | tf_op jit(solution)/shard_map/psum | solution.py:212
  1269.4 15.2 collective-permute-start.38
  1306.4 18.2 %all_to_all.46 = bf16[16,16,256]{2,1,0:T(8,128)(2,1)S(1)} all-to-all(bf16[16,16,256]{2,1,0:T(8,128)(2,1)S(1)} %bitcast.307), channel_id=1, replica_groups=mesh['row'=16,'col'=32] {'row'}, dimensions={0} | all-to-all | bytes 262144 | tf_op jit(solution)/shard_map/all_to_all | solution.py:203
  1326.6 123.0 %all-reduce.24.cloned.1.call-done = bf16[256,256]{0,1:T(8,128)(2,1)} async-done(((bf16[256,256]{0,1:T(8,128)(2,1)}), bf16[256,256]{0,1:T(8,128)(2,1)}) %all-reduce.24.cloned.1.call-update) | async-done | bytes 131088 | tf_op jit(solution)/shard_map/psum | solution.py:212
  1461.4 13.9 collective-permute-start.45
  1490.9 19.0 %all_to_all.47 = bf16[16,8,256]{2,1,0:T(8,128)(2,1)S(1)} all-to-all(bf16[16,8,256]{2,1,0:T(8,128)(2,1)S(1)} %bitcast.308), channel_id=1, replica_groups=mesh['row'=16,'col'=32] {'row'}, dimensions={0} | all-to-all | bytes 131072 | tf_op jit(solution)/shard_map/all_to_all | solution.py:203
  1511.7 120.9 %all-reduce.26.cloned.1.call-done = bf16[256,256]{0,1:T(8,128)(2,1)} async-done(((bf16[256,256]{0,1:T(8,128)(2,1)}), bf16[256,256]{0,1:T(8,128)(2,1)}) %all-reduce.26.cloned.1.call-update) | async-done | bytes 131088 | tf_op jit(solution)/shard_map/psum | solution.py:212
  1638.6 12.4 collective-permute-start.50
  (400 shorter events, 305.6 us)
Async XLA Ops:
  7.2 172.1 %all-reduce.12.cloned.1.call-start = ((), (), s32[]{:S(2)}) async-start(), calls=%async_computation.9 | async-start | bytes 262144 | tf_op jit(solution)/shard_map/psum | solution.py:154
  7.2 40.5 %collective-permute-start.5 = (bf16[64,64]{1,0:T(8,128)(2,1)}, bf16[64,64]{1,0:T(8,128)(2,1)S(1)}, u32[]{:S(2)}, u32[]{:S(2)}) collective-permute-start(bf16[64,64]{1,0:T(8,128)(2,1)} %param.24), channel_id=1, source_target_pairs={{0,1},{1,0},{2,3},{3,2},{4,5},{5,4},{6,7},{7,6},{8,9},{9,8},{10,11... | collective-permute-start | bytes 24584 | tf_op jit(solution)/shard_map/ppermute | solution.py:10
  16.0 219.1 %collective-permute-start.12 = (bf16[128,32]{0,1:T(8,128)(2,1)}, bf16[128,32]{0,1:T(8,128)(2,1)S(1)}, u32[]{:S(2)}, u32[]{:S(2)}) collective-permute-start(bf16[128,32]{0,1:T(8,128)(2,1)} %param.23), channel_id=1, source_target_pairs={{0,1},{1,0},{2,3},{3,2},{4,5},{5,4},{6,7},{7,6},{8,9},{9,8},{10,11... | collective-permute-start | bytes 24584 | tf_op jit(solution)/shard_map/ppermute | solution.py:10
  18.0 466.2 %collective-permute-start.22 = (bf16[192,16]{0,1:T(8,128)(2,1)}, bf16[192,16]{0,1:T(8,128)(2,1)S(1)}, u32[]{:S(2)}, u32[]{:S(2)}) collective-permute-start(bf16[192,16]{0,1:T(8,128)(2,1)} %param.22), channel_id=1, source_target_pairs={{0,1},{1,0},{2,3},{3,2},{4,5},{5,4},{6,7},{7,6},{8,9},{9,8},{10,11... | collective-permute-start | bytes 18440 | tf_op jit(solution)/shard_map/ppermute | solution.py:10
  20.4 725.6 %collective-permute-start = (bf16[256,8]{0,1:T(8,128)(2,1)}, bf16[256,8]{0,1:T(8,128)(2,1)S(1)}, u32[]{:S(2)}, u32[]{:S(2)}) collective-permute-start(bf16[256,8]{0,1:T(8,128)(2,1)} %param.21), channel_id=1, source_target_pairs={{0,1},{1,0},{2,3},{3,2},{4,5},{5,4},{6,7},{7,6},{8,9},{9,8},{10,11... | collective-permute-start | bytes 12296 | tf_op jit(solution)/shard_map/ppermute | solution.py:10
  185.4 16.8 %collective-permute-start.8 = (bf16[64,64]{1,0:T(8,128)(2,1)S(1)}, bf16[64,64]{1,0:T(8,128)(2,1)S(1)}, u32[]{:S(2)}, u32[]{:S(2)}) collective-permute-start(bf16[64,64]{1,0:T(8,128)(2,1)S(1)} %select_convert_fusion.14), channel_id=1, source_target_pairs={{0,1},{1,0},{2,3},{3,2},{4,5},{5,4},{6,7},{7,6},{8,9},{9,8},{10,11... | collective-permute-start | bytes 24584 | tf_op jit(solution)/shard_map/ppermute | solution.py:10
  218.2 27.5 %all-to-all-start = ((bf16[16,8,256]{2,1,0:T(8,128)(2,1)}), bf16[16,8,256]{2,1,0:T(8,128)(2,1)S(1)}, u32[]{:S(2)}, u32[]{:S(2)}) async-start(bf16[16,8,256]{2,1,0:T(8,128)(2,1)} %scatter_fusion), calls=%async_computation | async-start | bytes 131072 | tf_op jit(solution)/shard_map/all_to_all | solution.py:170
  235.1 22.1 %collective-permute-start.13 = (bf16[128,64]{0,1:T(8,128)(2,1)S(1)}, bf16[128,64]{0,1:T(8,128)(2,1)S(1)}, u32[]{:S(2)}, u32[]{:S(2)}) collective-permute-start(bf16[128,64]{0,1:T(8,128)(2,1)S(1)} %maximum_select_fusion.28), channel_id=1, source_target_pairs={{0,2},{1,3},{2,0},{3,1},{4,6},{5,7},{6,4},{7,5},{8,10},{9,11},{10,... | collective-permute-start | bytes 49160 | tf_op jit(solution)/shard_map/ppermute | solution.py:10
  245.7 26.6 %all-to-all-start.1 = ((bf16[16,8,256]{2,1,0:T(8,128)(2,1)}), bf16[16,8,256]{2,1,0:T(8,128)(2,1)S(1)}, u32[]{:S(2)}, u32[]{:S(2)}) async-start(bf16[16,8,256]{2,1,0:T(8,128)(2,1)} %scatter_fusion.1), calls=%async_computation.1 | async-start | bytes 131072 | tf_op jit(solution)/shard_map/all_to_all | solution.py:177
  257.1 146.0 %all-reduce.14.cloned.1.call-start = ((), (), s32[]{:S(2)}) async-start(), calls=%async_computation.10 | async-start | bytes 262144 | tf_op jit(solution)/shard_map/psum | solution.py:154
  257.2 16.7 %collective-permute-start.14 = (bf16[128,128]{0,1:T(8,128)(2,1)S(1)}, bf16[128,128]{0,1:T(8,128)(2,1)S(1)}, u32[]{:S(2)}, u32[]{:S(2)}) collective-permute-start(bf16[128,128]{0,1:T(8,128)(2,1)S(1)} %maximum_select_fusion.23), channel_id=1, source_target_pairs={{0,4},{1,5},{2,6},{3,7},{4,0},{5,1},{6,2},{7,3},{8,12},{9,13},{10,... | collective-permute-start | bytes 98312 | tf_op jit(solution)/shard_map/ppermute | solution.py:10
  415.0 14.7 collective-permute-start.17
  429.7 10.4 collective-permute-start.18
  444.6 12.9 collective-permute-start.20
  473.2 28.5 %all-to-all-start.2 = ((bf16[16,16,256]{2,1,0:T(8,128)(2,1)}), bf16[16,16,256]{2,1,0:T(8,128)(2,1)S(1)}, u32[]{:S(2)}, u32[]{:S(2)}) async-start(bf16[16,16,256]{2,1,0:T(8,128)(2,1)} %scatter_fusion.2), calls=%async_computation.2 | async-start | bytes 262144 | tf_op jit(solution)/shard_map/all_to_all | solution.py:170
  501.7 28.9 %all-to-all-start.3 = ((bf16[16,16,256]{2,1,0:T(8,128)(2,1)}), bf16[16,16,256]{2,1,0:T(8,128)(2,1)S(1)}, u32[]{:S(2)}, u32[]{:S(2)}) async-start(bf16[16,16,256]{2,1,0:T(8,128)(2,1)} %scatter_fusion.3), calls=%async_computation.3 | async-start | bytes 262144 | tf_op jit(solution)/shard_map/all_to_all | solution.py:177
  513.4 149.4 %all-reduce.16.cloned.1.call-start = ((), (), s32[]{:S(2)}) async-start(), calls=%async_computation.11 | async-start | bytes 196608 | tf_op jit(solution)/shard_map/psum | solution.py:154
  680.8 16.1 collective-permute-start.29
  739.3 44.1 %all-to-all-start.4 = ((bf16[16,24,256]{2,1,0:T(8,128)(2,1)}), bf16[16,24,256]{2,1,0:T(8,128)(2,1)S(1)}, u32[]{:S(2)}, u32[]{:S(2)}) async-start(bf16[16,24,256]{2,1,0:T(8,128)(2,1)} %scatter_fusion.4), calls=%async_computation.4 | async-start | bytes 393216 | tf_op jit(solution)/shard_map/all_to_all | solution.py:170
  751.2 9.3 collective-permute-start.34
  755.9 51.2 %collective-permute-start.2 = (bf16[256,32]{1,0:T(8,128)(2,1)S(1)}, bf16[256,32]{1,0:T(8,128)(2,1)S(1)}, u32[]{:S(2)}, u32[]{:S(2)}) collective-permute-start(bf16[256,32]{1,0:T(8,128)(2,1)S(1)} %broadcast_select_fusion), channel_id=1, source_target_pairs={{0,4},{1,5},{2,6},{3,7},{4,0},{5,1},{6,2},{7,3},{8,12},{9,13},{10,... | collective-permute-start | bytes 49160 | tf_op jit(solution)/shard_map/ppermute | solution.py:10
  783.5 44.9 %all-to-all-start.5 = ((bf16[16,24,256]{2,1,0:T(8,128)(2,1)}), bf16[16,24,256]{2,1,0:T(8,128)(2,1)S(1)}, u32[]{:S(2)}, u32[]{:S(2)}) async-start(bf16[16,24,256]{2,1,0:T(8,128)(2,1)} %scatter_fusion.5), calls=%async_computation.5 | async-start | bytes 393216 | tf_op jit(solution)/shard_map/all_to_all | solution.py:177
  795.1 163.9 %all-reduce.18.cloned.1.call-start = ((), (), s32[]{:S(2)}) async-start(), calls=%async_computation.12 | async-start | bytes 131072 | tf_op jit(solution)/shard_map/psum | solution.py:154
  807.2 14.1 collective-permute-start.3
  821.4 9.8 collective-permute-start.4
  832.1 267.3 %all-reduce.20.cloned.1.call-start = ((), (), s32[]{:S(2)}) async-start(), calls=%async_computation.13 | async-start | bytes 262144 | tf_op jit(solution)/shard_map/psum | solution.py:216
  960.8 290.6 %all-reduce.22.cloned.1.call-start = ((), (), s32[]{:S(2)}) async-start(), calls=%async_computation.14 | async-start | bytes 196608 | tf_op jit(solution)/shard_map/psum | solution.py:212
  1130.0 319.6 %all-reduce.24.cloned.1.call-start = ((), (), s32[]{:S(2)}) async-start(), calls=%async_computation.15 | async-start | bytes 262144 | tf_op jit(solution)/shard_map/psum | solution.py:212
  1269.4 16.1 collective-permute-start.38
  1326.6 305.9 %all-reduce.26.cloned.1.call-start = ((), (), s32[]{:S(2)}) async-start(), calls=%async_computation.16 | async-start | bytes 262144 | tf_op jit(solution)/shard_map/psum | solution.py:212
  1461.4 14.7 collective-permute-start.45
  1638.6 14.3 collective-permute-start.50
  (56 other events, 1490.0 us)
Sparse Core Ops, SparseCore 0:
  53.8 125.3 all-reduce.11
  275.6 127.4 all-reduce.13
  534.5 128.1 all-reduce.15
  832.3 126.7 all-reduce.17
  962.1 137.2 all-reduce.19
  1130.1 121.2 all-reduce.21
  1326.7 122.8 all-reduce.23
  1511.8 120.6 all-reduce.25
where the time goes:
time: 1670 us; the launch traced here: 1660 us
  waiting for transfers between devices  1060 us (63%)
  starting transfers between devices  293 us (18%)
  local copies, waits for them, and re-layouts  167 us (10%)
  blocking collectives  61.5 us (4%)
  other arithmetic  46.3 us (3%)
    psum x4, waiting for transfers between devices, per_device(): solved = lax.psum(partial_value.astype(jnp.bfloat16), 'row')  507 us
    psum x3, waiting for transfers between devices, per_device(): lax.psum(coupling_term.astype(jnp.bfloat16), 'row').astype(jnp.float32)  365 us
    ppermute x51, starting transfers between devices, swapped(): return lax.ppermute(value, axis, pairs)  236 us
    psum x1, waiting for transfers between devices, per_device(): summed = lax.psum(contribution.astype(jnp.bfloat16), 'col')  139 us
    scatter x6, local copies, waits for them, and re-layouts, pack_rows(): return buffer.at[local_target, local_slots].set(values)  89.6 us
    all_to_all x3, blocking collectives, per_device(): lax.all_to_all(parent_rows[own_lookup], 'row', split_axis=0, concat_axis=...  61.5 us
    unnamed x56, local copies, waits for them, and re-layouts  56.3 us
    ppermute x51, waiting for transfers between devices, swapped(): return lax.ppermute(value, axis, pairs)  51 us
  transfers between devices with their start and end apart: 65, of which 42 were waited for; matrix products, arithmetic and copies ran while one was open for 12% of the time, Pallas kernels for 0%

commit v1 on v0

v1 whole, which is shorter than its diff:
```python
import jax
import jax.numpy as jnp
from jax import lax
from jax.sharding import PartitionSpec as P

BF16 = jnp.bfloat16
F32 = jnp.float32
LANES = 128


def core_swapped(value):
    return lax.ppermute(value, "col", [(source, source ^ 1) for source in range(32)])


def chip_groups(bits):
    chips = 1 << bits
    return [
        [2 * (base + chip) + core for chip in range(chips)]
        for base in range(0, 16, chips)
        for core in range(2)
    ]


def summed_over_chips(value, bits):
    chips = 1 << bits
    copies = jnp.broadcast_to(value.astype(BF16)[None], (chips, *value.shape))
    got = lax.all_to_all(
        copies, "col", split_axis=0, concat_axis=0, tiled=True, axis_index_groups=chip_groups(bits)
    )
    return jnp.sum(got.astype(F32), axis=0)


def halves(block, core):
    half = block.shape[0] // 2
    first, second = block[:half], block[half:]
    return jnp.where(core == 0, first, second), jnp.where(core == 0, second, first)


def side_by_side(mine, other, core):
    return jnp.where(
        core == 0,
        jnp.concatenate([mine, other], axis=-1),
        jnp.concatenate([other, mine], axis=-1),
    )


def to_strips(block):
    return [block[:, at : at + LANES] for at in range(0, block.shape[1], LANES)]


def dot(left, right):
    return lax.dot_general(left, right, (((1,), (0,)), ((), ())), preferred_element_type=F32)


def dot_t(left, right):
    return lax.dot_general(left, right, (((1,), (1,)), ((), ())), preferred_element_type=F32)


def composite_targets(maps, fronts, orders, core):
    tables = [None] * 4
    for level in (1, 2, 3):
        parent = orders[level - 1]
        own = lax.dynamic_index_in_dim(maps[level], fronts[level], 0, keepdims=False)
        block = parent // 16
        half = block // 2
        at = jnp.minimum(own, parent - 1)
        inside = at % block
        place = jnp.where(inside // half == core, at // block * half + inside % half, -1)
        if level > 1:
            above = tables[level - 1]
            further = above[jnp.clip(own - parent, 0, parent - 1)]
            further = jnp.where(further >= 0, further + parent // 2, -1)
            place = jnp.where(own < parent, place, further)
        tables[level] = place
    return tables


def per_device(
    inverse_top,
    inverse_one,
    inverse_two,
    inverse_leaf,
    coupling_one,
    coupling_two,
    coupling_leaf,
    rhs_top,
    rhs_one,
    rhs_two,
    rhs_leaf,
    parent_map_one,
    parent_map_two,
    parent_map_leaf,
):
    row = lax.axis_index("row")
    column = lax.axis_index("col")
    core = column % 2
    inverses = [inverse_top, inverse_one, inverse_two, inverse_leaf]
    couplings = [None, coupling_one, coupling_two, coupling_leaf]
    right_sides = [rhs_top, rhs_one, rhs_two, rhs_leaf]
    maps = [None, parent_map_one, parent_map_two, parent_map_leaf]
    groups = [32, 16, 8, 4]
    orders = [inverse.shape[1] * 16 for inverse in inverses]
    fronts = [column // group for group in groups]
    chip_bits = [4, 3, 2, 1]

    blocks = [inverse.T for inverse in inverses] + couplings[1:]
    kept, sent = zip(*[halves(block, core) for block in blocks])
    rhs_kept, rhs_sent = zip(*[halves(block, core) for block in right_sides])
    got = core_swapped(list(sent) + list(rhs_sent))
    paired = [side_by_side(mine, other, core) for mine, other in zip(kept, got[:7])]
    rhs_paired = [side_by_side(mine, other, core) for mine, other in zip(rhs_kept, got[7:])]

    strips = [to_strips(block) for block in paired]
    packed = jnp.concatenate([piece for pieces in strips for piece in pieces], axis=0)
    gathered = lax.all_gather(packed, "row", axis=0)
    whole, at = [], 0
    for pieces in strips:
        depth = pieces[0].shape[0]
        parts = []
        for _ in pieces:
            parts.append(gathered[:, at : at + depth].reshape(16 * depth, LANES))
            at += depth
        whole.append(jnp.concatenate(parts, axis=1))
    solve = whole[:4]

    outgoing = []
    for level in range(4):
        block = rhs_paired[level]
        planes = block.shape[1] // 16
        spread = block.T.reshape(planes, 16, block.shape[0])
        chip = column % groups[level] // 2
        outgoing.append(
            lax.dynamic_update_slice(
                jnp.zeros((16, 16, block.shape[0]), BF16), spread, (chip * planes, 0, 0)
            )
        )
    incoming = lax.all_to_all(
        jnp.concatenate(outgoing, axis=2), "row", split_axis=0, concat_axis=0, tiled=True
    )
    total, at = [], 0
    for level in range(4):
        depth = rhs_paired[level].shape[0]
        part = incoming[:, :, at : at + depth].transpose(1, 0, 2)
        total.append(part.reshape(16, 16 * depth).astype(F32))
        at += depth

    targets = composite_targets(maps, fronts, orders, core)
    placed = [None]
    for level in (1, 2, 3):
        mine = whole[3 + level]
        other = core_swapped(mine)
        height = orders[level] // 2
        block = orders[level] // 16
        cut = targets[level].reshape(16, 2, block // 2)
        here = jnp.where(core == 0, cut[:, 0], cut[:, 1]).reshape(height)
        there = jnp.where(core == 0, cut[:, 1], cut[:, 0]).reshape(height)
        rows = sum(orders[:level]) // 2
        hot = lax.broadcasted_iota(jnp.int32, (rows, 2 * height), 0) == jnp.concatenate([here, there])[None]
        both = jnp.concatenate([mine, other], axis=0)
        placed.append(dot(hot.astype(BF16), both).astype(BF16))

    solved = [None] * 4
    for level in (3, 2, 1, 0):
        separator = summed_over_chips(total[level], chip_bits[level]).astype(BF16)
        partial = dot(separator, solve[level])
        solved[level] = partial + core_swapped(partial)
        if level > 0:
            contribution = dot_t(solved[level].astype(BF16), placed[level])
            at = 0
            for above in range(level - 1, -1, -1):
                height = orders[above] // 2
                total[above] = total[above] - contribution[:, at : at + height]
                at += height

    solutions = [None] * 4
    above = None
    for level in range(4):
        residual = solved[level].astype(BF16)
        if level > 0:
            partial = dot(above, placed[level])
            residual = (residual.astype(F32) - (partial + core_swapped(partial))).astype(BF16)
        product = dot_t(residual, solve[level])
        solutions[level] = summed_over_chips(product, chip_bits[level]).astype(BF16)
        above = solutions[0] if level == 0 else jnp.concatenate([solutions[level], above], axis=1)

    sending = [value.reshape(16, 16, -1).transpose(1, 0, 2) for value in solutions]
    returned = lax.all_to_all(
        jnp.concatenate(sending, axis=2), "row", split_axis=0, concat_axis=0, tiled=True
    )
    kept, sent, at = [], [], 0
    for level in range(4):
        depth = sending[level].shape[2]
        planes = 32 // groups[level]
        chip = column % groups[level] // 2
        part = lax.dynamic_slice(
            returned[:, :, at : at + depth], (chip * planes, 0, 0), (planes, 16, depth)
        )
        mine, other = halves(part.reshape(planes * 16, depth), core)
        kept.append(mine)
        sent.append(other)
        at += depth
    got = core_swapped(sent)
    results = [side_by_side(mine, other, core).T for mine, other in zip(kept, got)]
    return tuple(results)


def solution(mesh):
    split = P("row", "col")
    in_specs = (P("col", "row"),) * 4 + (split,) * 7 + (P(),) * 3
    return jax.shard_map(
        per_device, mesh=mesh, in_specs=in_specs, out_specs=(split,) * 4, check_vma=False
    )
```

time: 1670 us -> 351 us (0.21)
  waiting for transfers between devices: 1060 us -> 87 us
  starting transfers between devices: 293 us -> 113 us
  local copies, waits for them, and re-layouts: 167 us -> 43.1 us
  other arithmetic: 46.3 us -> 14.4 us
  blocking collectives: 61.5 us -> 36.8 us
  matrix products: 14.1 us -> 38.2 us
    psum x8 -> x0, waiting for transfers between devices: 1010 us -> none  [the longest x4 507 us: per_device(): solved = lax.psum(partial_value.astype(jnp.bfloat16), 'row')]
    ppermute x51 -> x25, starting transfers between devices: 236 us -> 76.6 us  [core_swapped(): lax.ppermute(value, 'col', [(source, source ^ 1) for source in range(32)])]
    scatter x12 -> x0, local copies, waits for them, and re-layouts: 90.1 us -> none  [the longest x6 89.6 us: pack_rows(): return buffer.at[local_target, local_slots].set(values)]
    all_to_all x6 -> x7, waiting for transfers between devices: 0.02 us -> 55.6 us  [the longest x5 28.1 us: summed_over_chips(): lax.all_to_all(copies, 'col', split_axis=0, concat_axis=0, tiled=True, ax...]
    unnamed x56 -> x94, local copies, waits for them, and re-layouts: 56.3 us -> 7.41 us
    ppermute x51 -> x25, waiting for transfers between devices: 51 us -> 4.33 us  [core_swapped(): lax.ppermute(value, 'col', [(source, source ^ 1) for source in range(32)])]
    another operation x12 -> x0, other arithmetic: 27.1 us -> none
    all_gather x0 -> x1, waiting for transfers between devices: none -> 27 us  [per_device(): gathered = lax.all_gather(packed, 'row', axis=0)]
  transfers between devices with their start and end apart: 65 -> 33, of which waited for: 42 -> 14; matrix products, arithmetic and copies ran while one was open for 12% -> 21% of each run, Pallas kernels for 0% -> 0%
where the time goes in v1:
time: 351 us; the launch traced here: 348 us
  starting transfers between devices  113 us (32%)
  waiting for transfers between devices  87 us (25%)
  local copies, waits for them, and re-layouts  43.1 us (12%)
  matrix products  38.2 us (11%)
  blocking collectives  36.8 us (10%)
  between operations  15.7 us (4%)
  other arithmetic  14.4 us (4%)
    ppermute x25, starting transfers between devices, core_swapped(): lax.ppermute(value, 'col', [(source, source ^ 1) for source in range(32)])  76.6 us
    all_to_all x3, blocking collectives, summed_over_chips(): lax.all_to_all(copies, 'col', split_axis=0, concat_axis=0, tiled=True, ax...  36.8 us
    dot_general x10, matrix products, dot(): lax.dot_general(left, right, (((1,), (0,)), ((), ())), preferred_element_...  31.9 us
    all_to_all x5, waiting for transfers between devices, summed_over_chips(): lax.all_to_all(copies, 'col', split_axis=0, concat_axis=0, tiled=True, ax...  28.1 us
    all_gather x1, waiting for transfers between devices, per_device(): gathered = lax.all_gather(packed, 'row', axis=0)  27 us
    all_to_all x5, starting transfers between devices, summed_over_chips(): lax.all_to_all(copies, 'col', split_axis=0, concat_axis=0, tiled=True, ax...  18.8 us
    gather x2, local copies, waits for them, and re-layouts, composite_targets(): further = above[jnp.clip(own - parent, 0, parent - 1)]  17.9 us
    all_to_all x1, waiting for transfers between devices, per_device(): lax.all_to_all(jnp.concatenate(outgoing, axis=2), 'row', split_axis=0, co...  15.1 us
  transfers between devices with their start and end apart: 33, of which 14 were waited for; matrix products, arithmetic and copies ran while one was open for 21% of the time, Pallas kernels for 0%

profile of v1, /device:TPU:1, one launch (start us, length us, event | category | flops | bytes accessed | tf_op | source)
XLA Modules:
  0.0 348.2 jit_solution(7780298180870203795)
XLA Ops:
  8.0 8.8 %collective-permute-start.7 = (bf16[32,256]{1,0:T(8,128)(2,1)S(1)}, bf16[32,256]{1,0:T(8,128)(2,1)S(1)}, u32[]{:S(2)}, u32[]{:S(2)}) collective-permute-start(bf16[32,256]{1,0:T(8,128)(2,1)S(1)} %get-tuple-element.87), channel_id=1, source_target_pairs={{0,1},{1,0},{2,3},{3,2},{4,5},{5,4},{6,7},{7,6},{8,9},{9,8},{10,11... | collective-permute-start | bytes 49160 | tf_op jit(solution)/shard_map/ppermute | solution.py:12
  49.2 11.8 %gather_fusion = s32[2048]{0:T(1024)S(1)} fusion(s32[3072]{0:T(1024)S(1)} %fusion.63, s32[2048]{0:T(1024)S(1)} %broadcast_clamp_fusion), kind=kCustom, calls=%fused_computation | custom fusion | bytes 24576 | tf_op jit(solution)/shard_map/gather | solution.py:71
  62.6 6.2 %gather_fusion.1 = s32[1024]{0:T(1024)S(1)} fusion(s32[2048]{0:T(1024)S(1)} %get-tuple-element.95, s32[1024]{0:T(1024)S(1)} %broadcast_clamp_fusion.1), kind=kCustom, calls=%fused_computation.1 | custom fusion | bytes 12288 | tf_op jit(solution)/shard_map/gather | solution.py:71
  70.4 9.5 %all-to-all-start = ((bf16[16,16,320]{2,1,0:T(8,128)(2,1)}), bf16[16,16,320]{2,1,0:T(8,128)(2,1)S(1)}, u32[]{:S(2)}, u32[]{:S(2)}) async-start(bf16[16,16,320]{2,1,0:T(8,128)(2,1)} %pad_maximum_fusion.11), calls=%async_computation | async-start | bytes 393216 | tf_op jit(solution)/shard_map/all_to_all | solution.py:137
  81.6 15.1 %all-to-all-done = bf16[16,16,320]{2,1,0:T(8,128)(2,1)S(1)} async-done(((bf16[16,16,320]{2,1,0:T(8,128)(2,1)}), bf16[16,16,320]{2,1,0:T(8,128)(2,1)S(1)}, u32[]{:S(2)}, u32[]{:S(2)}) %all-to-all-start) | async-done | bytes 163872 | tf_op jit(solution)/shard_map/all_to_all | solution.py:137
  97.6 3.3 all-to-all-start.1
  104.0 27.0 %all-gather.3.cloned.1.call-done = bf16[25600,128]{1,0:T(8,128)(2,1)} async-done(((bf16[1600,128]{1,0:T(8,128)(2,1)}), bf16[25600,128]{1,0:T(8,128)(2,1)}) %all-gather.3.cloned.1.call-update) | async-done | bytes 6553616 | tf_op jit(solution)/shard_map/all_gather | solution.py:115
  132.7 4.0 %collective-permute-start.11 = (f32[16,512]{1,0:T(8,128)S(1)}, f32[16,512]{1,0:T(8,128)S(1)}, u32[]{:S(2)}, u32[]{:S(2)}) collective-permute-start(f32[16,512]{1,0:T(8,128)S(1)} %fusion.51), channel_id=1, source_target_pairs={{0,1},{1,0},{2,3},{3,2},{4,5},{5,4},{6,7},{7,6},{8,9},{9,8},{10,11... | collective-permute-start | bytes 98312 | tf_op jit(solution)/shard_map/ppermute | solution.py:12
  138.7 2.7 fusion.101
  145.1 5.3 %fusion.6 = bf16[4608,512]{1,0:T(8,128)(2,1)S(1)} fusion(s32[1024]{0:T(1024)S(1)} %pad_add_fusion.2, bf16[512,512]{1,0:T(8,128)(2,1)S(1)} %collective-permute-done.12, bf16[512,128]{1,0:T(8,128)(2,1)S(1)} %bitcast.138, bf16[512,128]{1,0:T(8,128)(2,1)S(1)} %bitcast.140, bf16[512,128]{1,0:T(8,128)(2,1)S(1)} %bitcast.142, bf16[512,128]{1,0:T(8,128)(2,1)S(1)} %bitcast.136), kind=kOutput, calls=%fused_computation.11 | convolution fusion | flops 4844158976 | bytes 5771264 | tf_op jit(solution)/shard_map/dot_general | solution.py:52
  153.3 3.9 %all-to-all-start.2 = ((bf16[4,16,1024]{2,1,0:T(8,128)(2,1)}), bf16[4,16,1024]{2,1,0:T(8,128)(2,1)S(1)}, u32[]{:S(2)}, u32[]{:S(2)}) async-start(bf16[4,16,1024]{2,1,0:T(8,128)(2,1)} %broadcast_in_dim.40), calls=%async_computation.2 | async-start | bytes 262144 | tf_op jit(solution)/shard_map/all_to_all | solution.py:27
  157.2 2.8 fusion.100
  162.4 3.3 collective-permute-start.13
  168.1 9.2 %fusion.7 = bf16[3584,512]{1,0:T(8,128)(2,1)S(1)} fusion(s32[2048]{0:T(1024)S(1)} %copy-done.30, bf16[1024,512]{1,0:T(8,128)(2,1)} %collective-permute-done.14, bf16[1024,128]{1,0:T(8,128)(2,1)S(1)} %bitcast.126, bf16[1024,128]{1,0:T(8,128)(2,1)S(1)} %bitcast.128, bf16[1024,128]{1,0:T(8,128)(2,1)S(1)} %bitcast.130, bf16[1024,128]{1,0:T(8,128)(2,1)S(1)} %bitcast.124), kind=kOutput, calls=%fused_computation.12 | convolution fusion | flops 7535853568 | bytes 5775360 | tf_op jit(solution)/shard_map/dot_general | solution.py:52
  181.0 3.5 all-to-all-start.3
  184.8 6.6 %all-to-all-done.3 = bf16[8,16,1536]{2,1,0:T(8,128)(2,1)S(1)} async-done(((bf16[8,16,1536]{2,1,0:T(8,128)(2,1)}), bf16[8,16,1536]{2,1,0:T(8,128)(2,1)S(1)}, u32[]{:S(2)}, u32[]{:S(2)}) %all-to-all-start.3) | async-done | bytes 393248 | tf_op jit(solution)/shard_map/all_to_all | solution.py:27
  193.6 4.1 %collective-permute-start.15 = (f32[16,384]{1,0:T(8,128)S(1)}, f32[16,384]{1,0:T(8,128)S(1)}, u32[]{:S(2)}, u32[]{:S(2)}) collective-permute-start(f32[16,384]{1,0:T(8,128)S(1)} %fusion.35), channel_id=1, source_target_pairs={{0,1},{1,0},{2,3},{3,2},{4,5},{5,4},{6,7},{7,6},{8,9},{9,8},{10,11... | collective-permute-start | bytes 73736 | tf_op jit(solution)/shard_map/ppermute | solution.py:12
  197.7 8.1 %fusion.8 = bf16[2048,384]{1,0:T(8,128)(2,1)S(1)} fusion(s32[3072]{0:T(1024)S(1)} %pad_add_fusion, bf16[1536,384]{1,0:T(8,128)(2,1)} %collective-permute-done.16, bf16[1536,128]{1,0:T(8,128)(2,1)S(1)} %bitcast.120, bf16[1536,128]{1,0:T(8,128)(2,1)S(1)} %bitcast.122, bf16[1536,128]{1,0:T(8,128)(2,1)S(1)} %bitcast.118), kind=kOutput, calls=%fused_computation.13 | convolution fusion | flops 4848353280 | bytes 3944448 | tf_op jit(solution)/shard_map/dot_general | solution.py:52
  207.5 4.9 %all-to-all-start.4 = ((bf16[16,16,2048]{2,1,0:T(8,128)(2,1)}), bf16[16,16,2048]{2,1,0:T(8,128)(2,1)S(1)}, u32[]{:S(2)}, u32[]{:S(2)}) async-start(bf16[16,16,2048]{2,1,0:T(8,128)(2,1)} %broadcast_in_dim.42), calls=%async_computation.4 | async-start | bytes 2097152 | tf_op jit(solution)/shard_map/all_to_all | solution.py:27
  214.5 14.9 %all-to-all-done.4 = bf16[16,16,2048]{2,1,0:T(8,128)(2,1)S(1)} async-done(((bf16[16,16,2048]{2,1,0:T(8,128)(2,1)}), bf16[16,16,2048]{2,1,0:T(8,128)(2,1)S(1)}, u32[]{:S(2)}, u32[]{:S(2)}) %all-to-all-start.4) | async-done | bytes 1048608 | tf_op jit(solution)/shard_map/all_to_all | solution.py:27
  230.9 3.7 %collective-permute-start.17 = (f32[16,256]{1,0:T(8,128)S(1)}, f32[16,256]{1,0:T(8,128)S(1)}, u32[]{:S(2)}, u32[]{:S(2)}) collective-permute-start(f32[16,256]{1,0:T(8,128)S(1)} %fusion.34), channel_id=1, source_target_pairs={{0,1},{1,0},{2,3},{3,2},{4,5},{5,4},{6,7},{7,6},{8,9},{9,8},{10,11... | collective-permute-start | bytes 49160 | tf_op jit(solution)/shard_map/ppermute | solution.py:12
  236.9 19.2 %all_to_all.50 = bf16[16,16,2048]{2,1,0:T(8,128)(2,1)S(1)} all-to-all(bf16[16,16,2048]{2,1,0:T(8,128)(2,1)S(1)} %broadcast_in_dim.43), channel_id=1, replica_groups={{0,2,4,6,8,10,12,14,16,18,20,22,24,26,28,30},{1,3,5,7,9,11,13,15,17,19,..., dimensions={0} | all-to-all | bytes 2097152 | tf_op jit(solution)/shard_map/all_to_all | solution.py:27
  256.6 4.0 %collective-permute-start.18 = (f32[16,384]{1,0:T(8,128)S(1)}, f32[16,384]{1,0:T(8,128)S(1)}, u32[]{:S(2)}, u32[]{:S(2)}) collective-permute-start(f32[16,384]{1,0:T(8,128)S(1)} %fusion.106), channel_id=1, source_target_pairs={{0,1},{1,0},{2,3},{3,2},{4,5},{5,4},{6,7},{7,6},{8,9},{9,8},{10,11... | collective-permute-start | bytes 73736 | tf_op jit(solution)/shard_map/ppermute | solution.py:12
  262.9 10.4 %all_to_all.51 = bf16[8,16,1536]{2,1,0:T(8,128)(2,1)S(1)} all-to-all(bf16[8,16,1536]{2,1,0:T(8,128)(2,1)S(1)} %broadcast_in_dim.44), channel_id=1, replica_groups={{0,2,4,6,8,10,12,14},{1,3,5,7,9,11,13,15},{16,18,20,22,24,26,28,30},{17..., dimensions={0} | all-to-all | bytes 786432 | tf_op jit(solution)/shard_map/all_to_all | solution.py:27
  276.0 3.6 %collective-permute-start.19 = (f32[16,512]{1,0:T(8,128)S(1)}, f32[16,512]{1,0:T(8,128)S(1)}, u32[]{:S(2)}, u32[]{:S(2)}) collective-permute-start(f32[16,512]{1,0:T(8,128)S(1)} %fusion.46), channel_id=1, source_target_pairs={{0,1},{1,0},{2,3},{3,2},{4,5},{5,4},{6,7},{7,6},{8,9},{9,8},{10,11... | collective-permute-start | bytes 98312 | tf_op jit(solution)/shard_map/ppermute | solution.py:12
  280.9 7.2 %all_to_all.52 = bf16[4,16,1024]{2,1,0:T(8,128)(2,1)S(1)} all-to-all(bf16[4,16,1024]{2,1,0:T(8,128)(2,1)S(1)} %broadcast_in_dim.45), channel_id=1, replica_groups={{0,2,4,6},{1,3,5,7},{8,10,12,14},{9,11,13,15},{16,18,20,22},{17,19,21,2..., dimensions={0} | all-to-all | bytes 262144 | tf_op jit(solution)/shard_map/all_to_all | solution.py:27
  288.2 3.1 fusion.37
  291.3 3.4 collective-permute-start.20
  296.4 3.3 all-to-all-start.8
  303.5 8.0 %all-to-all-start.9 = ((bf16[16,16,320]{2,1,0:T(8,128)(2,1)}), bf16[16,16,320]{2,1,0:T(8,128)(2,1)S(1)}, u32[]{:S(2)}, u32[]{:S(2)}) async-start(bf16[16,16,320]{2,1,0:T(8,128)(2,1)} %copy.153), calls=%async_computation.9 | async-start | bytes 393216 | tf_op jit(solution)/shard_map/all_to_all | solution.py:187
  311.5 12.3 %all-to-all-done.9 = bf16[16,16,320]{2,1,0:T(8,128)(2,1)S(1)} async-done(((bf16[16,16,320]{2,1,0:T(8,128)(2,1)}), bf16[16,16,320]{2,1,0:T(8,128)(2,1)S(1)}, u32[]{:S(2)}, u32[]{:S(2)}) %all-to-all-start.9) | async-done | bytes 163872 | tf_op jit(solution)/shard_map/all_to_all | solution.py:187
  324.1 7.4 %collective-permute-start.24 = (bf16[64,32]{0,1:T(8,128)(2,1)S(1)}, bf16[64,32]{0,1:T(8,128)(2,1)S(1)}, u32[]{:S(2)}, u32[]{:S(2)}) collective-permute-start(bf16[64,32]{0,1:T(8,128)(2,1)S(1)} %copy.156), channel_id=1, source_target_pairs={{0,1},{1,0},{2,3},{3,2},{4,5},{5,4},{6,7},{7,6},{8,9},{9,8},{10,11... | collective-permute-start | bytes 12296 | tf_op jit(solution)/shard_map/ppermute | solution.py:12
  (281 shorter events, 91.9 us)
Async XLA Ops:
  7.2 123.8 %all-gather.3.cloned.1.call-start = ((), (), s32[]{:S(2)}) async-start(), calls=%async_computation.10 | async-start | bytes 6963200 | tf_op jit(solution)/shard_map/all_gather | solution.py:115
  8.0 22.8 %collective-permute-start.7 = (bf16[32,256]{1,0:T(8,128)(2,1)S(1)}, bf16[32,256]{1,0:T(8,128)(2,1)S(1)}, u32[]{:S(2)}, u32[]{:S(2)}) collective-permute-start(bf16[32,256]{1,0:T(8,128)(2,1)S(1)} %get-tuple-element.87), channel_id=1, source_target_pairs={{0,1},{1,0},{2,3},{3,2},{4,5},{5,4},{6,7},{7,6},{8,9},{9,8},{10,11... | collective-permute-start | bytes 49160 | tf_op jit(solution)/shard_map/ppermute | solution.py:12
  17.6 15.2 %collective-permute-start.10 = (bf16[32,256]{1,0:T(8,128)(2,1)S(1)}, bf16[32,256]{1,0:T(8,128)(2,1)S(1)}, u32[]{:S(2)}, u32[]{:S(2)}) collective-permute-start(bf16[32,256]{1,0:T(8,128)(2,1)S(1)} %get-tuple-element.85), channel_id=1, source_target_pairs={{0,1},{1,0},{2,3},{3,2},{4,5},{5,4},{6,7},{7,6},{8,9},{9,8},{10,11... | collective-permute-start | bytes 49160 | tf_op jit(solution)/shard_map/ppermute | solution.py:12
  20.5 14.8 %collective-permute-start.4 = (bf16[128,128]{1,0:T(8,128)(2,1)S(1)}, bf16[128,128]{1,0:T(8,128)(2,1)S(1)}, u32[]{:S(2)}, u32[]{:S(2)}) collective-permute-start(bf16[128,128]{1,0:T(8,128)(2,1)S(1)} %get-tuple-element.81), channel_id=1, source_target_pairs={{0,1},{1,0},{2,3},{3,2},{4,5},{5,4},{6,7},{7,6},{8,9},{9,8},{10,11... | collective-permute-start | bytes 98312 | tf_op jit(solution)/shard_map/ppermute | solution.py:12
  23.8 11.4 %collective-permute-start.6 = (bf16[64,256]{1,0:T(8,128)(2,1)S(1)}, bf16[64,256]{1,0:T(8,128)(2,1)S(1)}, u32[]{:S(2)}, u32[]{:S(2)}) collective-permute-start(bf16[64,256]{1,0:T(8,128)(2,1)S(1)} %get-tuple-element.79), channel_id=1, source_target_pairs={{0,1},{1,0},{2,3},{3,2},{4,5},{5,4},{6,7},{7,6},{8,9},{9,8},{10,11... | collective-permute-start | bytes 98312 | tf_op jit(solution)/shard_map/ppermute | solution.py:12
  26.5 8.8 %collective-permute-start.9 = (bf16[64,256]{1,0:T(8,128)(2,1)S(1)}, bf16[64,256]{1,0:T(8,128)(2,1)S(1)}, u32[]{:S(2)}, u32[]{:S(2)}) collective-permute-start(bf16[64,256]{1,0:T(8,128)(2,1)S(1)} %get-tuple-element.77), channel_id=1, source_target_pairs={{0,1},{1,0},{2,3},{3,2},{4,5},{5,4},{6,7},{7,6},{8,9},{9,8},{10,11... | collective-permute-start | bytes 98312 | tf_op jit(solution)/shard_map/ppermute | solution.py:12
  30.8 4.5 %collective-permute-start.5 = (bf16[96,192]{1,0:T(8,128)(2,1)S(1)}, bf16[96,192]{1,0:T(8,128)(2,1)S(1)}, u32[]{:S(2)}, u32[]{:S(2)}) collective-permute-start(bf16[96,192]{1,0:T(8,128)(2,1)S(1)} %get-tuple-element.67), channel_id=1, source_target_pairs={{0,1},{1,0},{2,3},{3,2},{4,5},{5,4},{6,7},{7,6},{8,9},{9,8},{10,11... | collective-permute-start | bytes 110600 | tf_op jit(solution)/shard_map/ppermute | solution.py:12
  32.8 3.3 collective-permute-start.8
  37.1 31.9 %collective-permute-start = (bf16[128,8]{0,1:T(8,128)(2,1)S(1)}, bf16[128,8]{0,1:T(8,128)(2,1)S(1)}, u32[]{:S(2)}, u32[]{:S(2)}) collective-permute-start(bf16[128,8]{0,1:T(8,128)(2,1)S(1)} %get-tuple-element.101), channel_id=1, source_target_pairs={{0,1},{1,0},{2,3},{3,2},{4,5},{5,4},{6,7},{7,6},{8,9},{9,8},{10,11... | collective-permute-start | bytes 6152 | tf_op jit(solution)/shard_map/ppermute | solution.py:12
  39.5 29.6 %collective-permute-start.1 = (bf16[96,16]{0,1:T(8,128)(2,1)S(1)}, bf16[96,16]{0,1:T(8,128)(2,1)S(1)}, u32[]{:S(2)}, u32[]{:S(2)}) collective-permute-start(bf16[96,16]{0,1:T(8,128)(2,1)S(1)} %get-tuple-element.97), channel_id=1, source_target_pairs={{0,1},{1,0},{2,3},{3,2},{4,5},{5,4},{6,7},{7,6},{8,9},{9,8},{10,11... | collective-permute-start | bytes 9224 | tf_op jit(solution)/shard_map/ppermute | solution.py:12
  41.5 27.6 %collective-permute-start.3 = (bf16[32,64]{1,0:T(8,128)(2,1)S(1)}, bf16[32,64]{1,0:T(8,128)(2,1)S(1)}, u32[]{:S(2)}, u32[]{:S(2)}) collective-permute-start(bf16[32,64]{1,0:T(8,128)(2,1)S(1)} %get-tuple-element.93), channel_id=1, source_target_pairs={{0,1},{1,0},{2,3},{3,2},{4,5},{5,4},{6,7},{7,6},{8,9},{9,8},{10,11... | collective-permute-start | bytes 12296 | tf_op jit(solution)/shard_map/ppermute | solution.py:12
  43.9 25.6 %collective-permute-start.2 = (bf16[64,32]{0,1:T(8,128)(2,1)S(1)}, bf16[64,32]{0,1:T(8,128)(2,1)S(1)}, u32[]{:S(2)}, u32[]{:S(2)}) collective-permute-start(bf16[64,32]{0,1:T(8,128)(2,1)S(1)} %get-tuple-element.99), channel_id=1, source_target_pairs={{0,1},{1,0},{2,3},{3,2},{4,5},{5,4},{6,7},{7,6},{8,9},{9,8},{10,11... | collective-permute-start | bytes 12296 | tf_op jit(solution)/shard_map/ppermute | solution.py:12
  70.4 26.3 %all-to-all-start = ((bf16[16,16,320]{2,1,0:T(8,128)(2,1)}), bf16[16,16,320]{2,1,0:T(8,128)(2,1)S(1)}, u32[]{:S(2)}, u32[]{:S(2)}) async-start(bf16[16,16,320]{2,1,0:T(8,128)(2,1)} %pad_maximum_fusion.11), calls=%async_computation | async-start | bytes 393216 | tf_op jit(solution)/shard_map/all_to_all | solution.py:137
  97.6 6.4 %all-to-all-start.1 = ((bf16[2,16,512]{2,1,0:T(8,128)(2,1)}), bf16[2,16,512]{2,1,0:T(8,128)(2,1)S(1)}, u32[]{:S(2)}, u32[]{:S(2)}) async-start(bf16[2,16,512]{2,1,0:T(8,128)(2,1)} %broadcast_in_dim.39), calls=%async_computation.1 | async-start | bytes 65536 | tf_op jit(solution)/shard_map/all_to_all | solution.py:27
  132.7 12.4 %collective-permute-start.11 = (f32[16,512]{1,0:T(8,128)S(1)}, f32[16,512]{1,0:T(8,128)S(1)}, u32[]{:S(2)}, u32[]{:S(2)}) collective-permute-start(f32[16,512]{1,0:T(8,128)S(1)} %fusion.51), channel_id=1, source_target_pairs={{0,1},{1,0},{2,3},{3,2},{4,5},{5,4},{6,7},{7,6},{8,9},{9,8},{10,11... | collective-permute-start | bytes 98312 | tf_op jit(solution)/shard_map/ppermute | solution.py:12
  136.8 8.3 %collective-permute-start.12 = (bf16[512,512]{1,0:T(8,128)(2,1)S(1)}, bf16[512,512]{1,0:T(8,128)(2,1)S(1)}, u32[]{:S(2)}, u32[]{:S(2)}) collective-permute-start(bf16[512,512]{1,0:T(8,128)(2,1)S(1)} %pad_maximum_fusion.8), channel_id=1, source_target_pairs={{0,1},{1,0},{2,3},{3,2},{4,5},{5,4},{6,7},{7,6},{8,9},{9,8},{10,11... | collective-permute-start | bytes 1572872 | tf_op jit(solution)/shard_map/ppermute | solution.py:12
  142.6 25.4 %collective-permute-start.14 = (bf16[1024,512]{1,0:T(8,128)(2,1)}, bf16[1024,512]{1,0:T(8,128)(2,1)}, u32[]{:S(2)}, u32[]{:S(2)}) collective-permute-start(bf16[1024,512]{1,0:T(8,128)(2,1)} %pad_maximum_fusion.3), channel_id=1, source_target_pairs={{0,1},{1,0},{2,3},{3,2},{4,5},{5,4},{6,7},{7,6},{8,9},{9,8},{10,11... | collective-permute-start | bytes 3145736 | tf_op jit(solution)/shard_map/ppermute | solution.py:12
  153.3 8.8 %all-to-all-start.2 = ((bf16[4,16,1024]{2,1,0:T(8,128)(2,1)}), bf16[4,16,1024]{2,1,0:T(8,128)(2,1)S(1)}, u32[]{:S(2)}, u32[]{:S(2)}) async-start(bf16[4,16,1024]{2,1,0:T(8,128)(2,1)} %broadcast_in_dim.40), calls=%async_computation.2 | async-start | bytes 262144 | tf_op jit(solution)/shard_map/all_to_all | solution.py:27
  162.4 5.6 %collective-permute-start.13 = (f32[16,512]{1,0:T(8,128)S(1)}, f32[16,512]{1,0:T(8,128)S(1)}, u32[]{:S(2)}, u32[]{:S(2)}) collective-permute-start(f32[16,512]{1,0:T(8,128)S(1)} %fusion.36), channel_id=1, source_target_pairs={{0,1},{1,0},{2,3},{3,2},{4,5},{5,4},{6,7},{7,6},{8,9},{9,8},{10,11... | collective-permute-start | bytes 98312 | tf_op jit(solution)/shard_map/ppermute | solution.py:12
  165.9 31.8 %collective-permute-start.16 = (bf16[1536,384]{1,0:T(8,128)(2,1)S(1)}, bf16[1536,384]{1,0:T(8,128)(2,1)}, u32[]{:S(2)}, u32[]{:S(2)}) collective-permute-start(bf16[1536,384]{1,0:T(8,128)(2,1)S(1)} %pad_maximum_fusion.1), channel_id=1, source_target_pairs={{0,1},{1,0},{2,3},{3,2},{4,5},{5,4},{6,7},{7,6},{8,9},{9,8},{10,11... | collective-permute-start | bytes 3538952 | tf_op jit(solution)/shard_map/ppermute | solution.py:12
  181.0 10.4 %all-to-all-start.3 = ((bf16[8,16,1536]{2,1,0:T(8,128)(2,1)}), bf16[8,16,1536]{2,1,0:T(8,128)(2,1)S(1)}, u32[]{:S(2)}, u32[]{:S(2)}) async-start(bf16[8,16,1536]{2,1,0:T(8,128)(2,1)} %broadcast_in_dim.41), calls=%async_computation.3 | async-start | bytes 786432 | tf_op jit(solution)/shard_map/all_to_all | solution.py:27
  193.6 12.3 %collective-permute-start.15 = (f32[16,384]{1,0:T(8,128)S(1)}, f32[16,384]{1,0:T(8,128)S(1)}, u32[]{:S(2)}, u32[]{:S(2)}) collective-permute-start(f32[16,384]{1,0:T(8,128)S(1)} %fusion.35), channel_id=1, source_target_pairs={{0,1},{1,0},{2,3},{3,2},{4,5},{5,4},{6,7},{7,6},{8,9},{9,8},{10,11... | collective-permute-start | bytes 73736 | tf_op jit(solution)/shard_map/ppermute | solution.py:12
  207.5 21.9 %all-to-all-start.4 = ((bf16[16,16,2048]{2,1,0:T(8,128)(2,1)}), bf16[16,16,2048]{2,1,0:T(8,128)(2,1)S(1)}, u32[]{:S(2)}, u32[]{:S(2)}) async-start(bf16[16,16,2048]{2,1,0:T(8,128)(2,1)} %broadcast_in_dim.42), calls=%async_computation.4 | async-start | bytes 2097152 | tf_op jit(solution)/shard_map/all_to_all | solution.py:27
  230.9 4.5 %collective-permute-start.17 = (f32[16,256]{1,0:T(8,128)S(1)}, f32[16,256]{1,0:T(8,128)S(1)}, u32[]{:S(2)}, u32[]{:S(2)}) collective-permute-start(f32[16,256]{1,0:T(8,128)S(1)} %fusion.34), channel_id=1, source_target_pairs={{0,1},{1,0},{2,3},{3,2},{4,5},{5,4},{6,7},{7,6},{8,9},{9,8},{10,11... | collective-permute-start | bytes 49160 | tf_op jit(solution)/shard_map/ppermute | solution.py:12
  256.6 4.8 %collective-permute-start.18 = (f32[16,384]{1,0:T(8,128)S(1)}, f32[16,384]{1,0:T(8,128)S(1)}, u32[]{:S(2)}, u32[]{:S(2)}) collective-permute-start(f32[16,384]{1,0:T(8,128)S(1)} %fusion.106), channel_id=1, source_target_pairs={{0,1},{1,0},{2,3},{3,2},{4,5},{5,4},{6,7},{7,6},{8,9},{9,8},{10,11... | collective-permute-start | bytes 73736 | tf_op jit(solution)/shard_map/ppermute | solution.py:12
  276.0 4.5 %collective-permute-start.19 = (f32[16,512]{1,0:T(8,128)S(1)}, f32[16,512]{1,0:T(8,128)S(1)}, u32[]{:S(2)}, u32[]{:S(2)}) collective-permute-start(f32[16,512]{1,0:T(8,128)S(1)} %fusion.46), channel_id=1, source_target_pairs={{0,1},{1,0},{2,3},{3,2},{4,5},{5,4},{6,7},{7,6},{8,9},{9,8},{10,11... | collective-permute-start | bytes 98312 | tf_op jit(solution)/shard_map/ppermute | solution.py:12
  291.3 4.2 %collective-permute-start.20 = (f32[16,512]{1,0:T(8,128)S(1)}, f32[16,512]{1,0:T(8,128)S(1)}, u32[]{:S(2)}, u32[]{:S(2)}) collective-permute-start(f32[16,512]{1,0:T(8,128)S(1)} %fusion.37), channel_id=1, source_target_pairs={{0,1},{1,0},{2,3},{3,2},{4,5},{5,4},{6,7},{7,6},{8,9},{9,8},{10,11... | collective-permute-start | bytes 98312 | tf_op jit(solution)/shard_map/ppermute | solution.py:12
  296.4 6.0 %all-to-all-start.8 = ((bf16[2,16,512]{2,1,0:T(8,128)(2,1)}), bf16[2,16,512]{2,1,0:T(8,128)(2,1)S(1)}, u32[]{:S(2)}, u32[]{:S(2)}) async-start(bf16[2,16,512]{2,1,0:T(8,128)(2,1)} %broadcast_in_dim.46), calls=%async_computation.8 | async-start | bytes 65536 | tf_op jit(solution)/shard_map/all_to_all | solution.py:27
  303.5 20.4 %all-to-all-start.9 = ((bf16[16,16,320]{2,1,0:T(8,128)(2,1)}), bf16[16,16,320]{2,1,0:T(8,128)(2,1)S(1)}, u32[]{:S(2)}, u32[]{:S(2)}) async-start(bf16[16,16,320]{2,1,0:T(8,128)(2,1)} %copy.153), calls=%async_computation.9 | async-start | bytes 393216 | tf_op jit(solution)/shard_map/all_to_all | solution.py:187
  324.1 16.7 %collective-permute-start.24 = (bf16[64,32]{0,1:T(8,128)(2,1)S(1)}, bf16[64,32]{0,1:T(8,128)(2,1)S(1)}, u32[]{:S(2)}, u32[]{:S(2)}) collective-permute-start(bf16[64,32]{0,1:T(8,128)(2,1)S(1)} %copy.156), channel_id=1, source_target_pairs={{0,1},{1,0},{2,3},{3,2},{4,5},{5,4},{6,7},{7,6},{8,9},{9,8},{10,11... | collective-permute-start | bytes 12296 | tf_op jit(solution)/shard_map/ppermute | solution.py:12
  331.5 8.2 %collective-permute-start.23 = (bf16[32,64]{1,0:T(8,128)(2,1)S(1)}, bf16[32,64]{1,0:T(8,128)(2,1)S(1)}, u32[]{:S(2)}, u32[]{:S(2)}) collective-permute-start(bf16[32,64]{1,0:T(8,128)(2,1)S(1)} %bitcast.184), channel_id=1, source_target_pairs={{0,1},{1,0},{2,3},{3,2},{4,5},{5,4},{6,7},{7,6},{8,9},{9,8},{10,11... | collective-permute-start | bytes 12296 | tf_op jit(solution)/shard_map/ppermute | solution.py:12
  333.5 4.4 %collective-permute-start.21 = (bf16[8,128]{1,0:T(8,128)(2,1)S(1)}, bf16[8,128]{1,0:T(8,128)(2,1)S(1)}, u32[]{:S(2)}, u32[]{:S(2)}) collective-permute-start(bf16[8,128]{1,0:T(8,128)(2,1)S(1)} %get-tuple-element.75), channel_id=1, source_target_pairs={{0,1},{1,0},{2,3},{3,2},{4,5},{5,4},{6,7},{7,6},{8,9},{9,8},{10,11... | collective-permute-start | bytes 6152 | tf_op jit(solution)/shard_map/ppermute | solution.py:12
  (34 other events, 464.9 us)
Sparse Core Ops, SparseCore 0:
  37.2 93.8 all-gather.2
